TPU v7x, 256 devices: a whole 4x4x8 slice. The times are simulated.
256 devices in a mesh: col: 64 (over y, z, core), row: 4 (over x).
Axes of the slice: x: 4, y: 4, z: 8, core: 2. Of those that a mesh axis runs over, the one named last changes fastest.
Arguments:
- tiles: bfloat16 [1024, 6, 256, 256], P('col', None, 'row'), may hold values from 0.049804688 to 1
- tile_rows: int32 [1024, 6], P('col'), may hold values from 0 to 1023, as said below
- keep: int32 [1024, 6], P('col'), may hold values from 0 to 1, as said below
- hand: int32 [64], P('col'), may hold values from 0 to 8, as said below
Outputs:
- columns: bfloat16 [1024, 6, 256, 256], P('col', None, 'row')
Inputs may be any that keep to these rules, and one draw needn't show every extreme that they name: `tile_rows`: slot 0 of column tile j is j itself; slots 1 to 3 are the other three column tiles of its aligned group of four on the same owner; slots 4 to 5 are column tiles of other owners, all distinct. The listing is symmetric: if k stands in slot s of j then j stands in slot s of k. For a k in slots 4 and up, the lists of j and k share only j and k. No owner lists more than (32 + 64 / 2 - 1) // (64 / 2) column tiles of one other owner, and some owner reaches that. `keep`: slot 0 is always kept. hand[d] equals hand[d + 64 / 2] for the first half of owners.
All inputs are finite; a program needn't handle non-finite values.
Results may differ from a plain program's by a relative error of at most 0.001.
Values may be sent and summed in bfloat16 or wider, within the bound.
A program may use at most 192 MiB of HBM per device.

v0:
```python
import jax
import jax.numpy as jnp
from jax import lax
from jax.sharding import PartitionSpec as P


def shifted(shard, axis, by):
    size = lax.axis_size(axis)
    return lax.ppermute(shard, axis, [(i, (i + by) % size) for i in range(size)])


def local(tiles, tile_rows, keep, hand):
    tile_count = tiles.shape[0]
    slot_count = tiles.shape[1]
    row_share = tiles.shape[2]
    tile_width = tiles.shape[3]
    axis_count = lax.axis_size("col")
    half_axis = axis_count // 2
    remote_count = slot_count - 4
    far_ids = tile_rows[:, 4:].reshape(-1)
    request_count = far_ids.shape[0]
    capacity = (request_count + half_axis - 1) // half_axis
    owners = far_ids // tile_count
    far_slot = far_ids % tile_count
    matching = jnp.tile(jnp.arange(remote_count, dtype=jnp.int32), tile_count)
    one_hot = (owners[:, None] == jnp.arange(axis_count, dtype=jnp.int32)[None, :]).astype(
        jnp.int32
    )
    earlier = jnp.cumsum(one_hot, 0) - one_hot
    order_in = jnp.sum(earlier * one_hot, 1)
    request_table = jnp.zeros((axis_count, capacity, 2), jnp.int32)
    request_table = request_table.at[owners, order_in].set(jnp.stack([far_slot, matching], 1))
    asked = lax.all_to_all(request_table, "col", split_axis=0, concat_axis=0, tiled=True)
    asked_slot = asked[:, :, 0]
    arrived, arrived_rows = (
        lax.all_to_all(tiles[asked_slot], "col", split_axis=0, concat_axis=0, tiled=True),
        lax.all_to_all(tile_rows[asked_slot], "col", split_axis=0, concat_axis=0, tiled=True),
    )
    far_tiles = arrived[owners, order_in]
    far_rows = arrived_rows[owners, order_in]
    fetched_width = far_tiles.shape[1]
    far_tiles = far_tiles.reshape(tile_count, remote_count, fetched_width, row_share, tile_width)
    far_rows = far_rows.reshape(tile_count, remote_count, fetched_width)
    near_slot = tile_rows[:, :4] % tile_count
    near_tiles = tiles[near_slot]
    near_rows = tile_rows[near_slot]

    def one_column(operands):
        near_here, near_list, far_here, far_list, own_list, own_piece = operands
        near_match = (near_list[None, :, :] == own_list[:, None, None]).astype(jnp.bfloat16)
        far_match = (far_list[None, :, :] == own_list[:, None, None]).astype(jnp.bfloat16)
        near_pick = jnp.einsum(
            "qst,strk->qsrk", near_match, near_here, preferred_element_type=jnp.float32
        )
        far_pick = jnp.einsum(
            "qst,strk->qsrk", far_match, far_here, preferred_element_type=jnp.float32
        )
        picked = jnp.concatenate([near_pick, far_pick], 1).astype(jnp.bfloat16)
        return jnp.einsum("qsrk,skc->qrc", picked, own_piece, preferred_element_type=jnp.float32)

    expanded = lax.map(
        one_column,
        (
            near_tiles,
            near_rows,
            far_tiles,
            far_rows,
            tile_rows,
            lax.all_gather(tiles, "row", axis=2, tiled=True),
        ),
    )
    expanded = expanded * keep.astype(jnp.float32)[:, :, None, None]
    inflated = expanded * expanded
    local_sums = jnp.sum(inflated, axis=(1, 2))
    column_sum = lax.psum(local_sums, "row")
    state = (tile_width * inflated / column_sum[:, None, None, :]).astype(jnp.bfloat16)
    position = jnp.arange(tile_count, dtype=jnp.int32)
    handed = position >= tile_count - hand[0]
    partner_state = shifted(state, "col", half_axis)
    return jnp.where(handed[:, None, None, None], partner_state, state)


def solution(mesh):
    placed = (P("col", None, "row", None), P("col", None), P("col", None), P("col"))
    return jax.shard_map(
        local, mesh=mesh, in_specs=placed, out_specs=P("col", None, "row", None), check_vma=False
    )
```

profile of v0, /device:TPU:1, one launch (start us, length us, event | category | flops | bytes accessed | tf_op | source)
XLA Modules:
  0.0 538.0 jit_solution(1530990392594931980)
XLA Ops:
  9.3 13.2 %all-to-all-start = ((s32[64,1,2]{2,1,0:T(1,128)}), s32[64,1,2]{2,1,0:T(1,128)S(1)}, u32[]{:S(2)}, u32[]{:S(2)}) async-start(s32[64,1,2]{2,1,0:T(1,128)} %bitcast.30), calls=%async_computation | async-start | bytes 65536 | tf_op jit(solution)/shard_map/all_to_all | solution.py:33
  23.2 8.4 %all-to-all-done = s32[64,1,2]{2,1,0:T(1,128)S(1)} async-done(((s32[64,1,2]{2,1,0:T(1,128)}), s32[64,1,2]{2,1,0:T(1,128)S(1)}, u32[]{:S(2)}, u32[]{:S(2)}) %all-to-all-start) | async-done | bytes 544 | tf_op jit(solution)/shard_map/all_to_all | solution.py:33
  34.1 4.7 all-to-all-start.2
  38.8 9.1 %gather_fusion.2 = bf16[64,6,64,256]{3,2,1,0:T(8,128)(2,1)} fusion(bf16[16,6,64,256]{3,2,1,0:T(8,128)(2,1)} %param.6, s32[1024]{0:T(1024)S(1)} %pad_clamp_fusion), kind=kCustom, calls=%fused_computation.2 | custom fusion | bytes 25166080 | tf_op jit(solution)/shard_map/gather | solution.py:36
  48.1 10.5 %all-to-all-start.1 = ((bf16[64,1,6,64,256]{4,3,2,1,0:T(8,128)(2,1)}), bf16[64,1,6,64,256]{4,3,2,1,0:T(8,128)(2,1)}, u32[]{:S(2)}, u32[]{:S(2)}) async-start(bf16[64,1,6,64,256]{4,3,2,1,0:T(8,128)(2,1)} %bitcast.80), calls=%async_computation.1 | async-start | bytes 25165824 | tf_op jit(solution)/shard_map/all_to_all | solution.py:36
  60.5 7.2 %gather_fusion = bf16[64,6,64,256]{3,2,1,0:T(8,128)(2,1)} fusion(bf16[16,6,64,256]{3,2,1,0:T(8,128)(2,1)S(1)} %copy-done, s32[1024]{0:T(1024)S(1)} %pad_clamp_fusion.1), kind=kCustom, calls=%fused_computation | custom fusion | bytes 25166080 | tf_op jit(solution)/shard_map/gather | solution.py:45
  67.7 14.5 %copy.39 = bf16[64,6,64,256]{3,1,2,0:T(8,128)(2,1)} copy(bf16[64,6,64,256]{3,2,1,0:T(8,128)(2,1)} %gather_fusion) | data formatting | bytes 25165824 | tf_op jit(solution)/shard_map/gather | solution.py:45
  82.9 251.4 %all-to-all-done.1 = bf16[64,1,6,64,256]{4,3,2,1,0:T(8,128)(2,1)} async-done(((bf16[64,1,6,64,256]{4,3,2,1,0:T(8,128)(2,1)}), bf16[64,1,6,64,256]{4,3,2,1,0:T(8,128)(2,1)}, u32[]{:S(2)}, u32[]{:S(2)}) %all-to-all-start.1) | async-done | bytes 12582944 | tf_op jit(solution)/shard_map/all_to_all | solution.py:36
  334.3 8.2 %gather_fusion.3 = bf16[32,6,64,256]{3,2,1,0:T(8,128)(2,1)} fusion(bf16[64,1,6,64,256]{4,3,2,1,0:T(8,128)(2,1)} %all-to-all-done.1, s32[32]{0:T(128)S(1)} %get-tuple-element.96), kind=kCustom, calls=%fused_computation.3 | custom fusion | bytes 12583168 | tf_op jit(solution)/shard_map/gather | solution.py:39
  342.5 93.7 %while.10 = (s32[]{:T(128)}, f32[16,6,64,256]{3,2,1,0:T(8,128)}, bf16[16,4,6,64,256]{4,2,3,1,0:T(8,128)(2,1)}, s32[16,4,6]{2,1,0:T(4,128)S(1)}, s32[16,6]{1,0:T(...) while((s32[]{:T(128)}, f32[16,6,64,256]{3,2,1,0:T(8,128)}, ...), condition=%wide.region_4.5_spmd, body=%wide.region_3.4_spmd.sunk | while | flops 310247648 | bytes 8128637 | solution.py:61
  346.1 2.4 fusion.46
  363.6 2.4 fusion.46
  381.2 2.4 fusion.46
  387.1 2.4 fusion.46
  416.3 2.4 fusion.46
  422.2 2.4 fusion.46
  428.0 2.4 fusion.46
  433.9 2.4 fusion.46
  436.3 3.6 fusion.20
  439.8 13.1 %psum.7 = f32[16,256]{1,0:T(8,128)S(1)} all-reduce(f32[16,256]{1,0:T(8,128)S(1)} %fusion.20), channel_id=1, replica_groups=mesh['col'=64,'row'=4] {'row'}, use_global_device_ids=true, to_apply=%region_6.7 | all-reduce | flops 4096 | bytes 32768 | tf_op jit(solution)/shard_map/psum | solution.py:75
  453.0 3.8 divide_convert_fusion
  456.8 3.1 collective-permute-start
  460.5 66.0 %collective-permute-done = bf16[16,6,64,256]{3,2,1,0:T(8,128)(2,1)S(1)} collective-permute-done((bf16[16,6,64,256]{3,2,1,0:T(8,128)(2,1)S(1)}, bf16[16,6,64,256]{3,2,1,0:T(8,128)(2,1)S(1)}, u32[]{:S(2)}, u32[]{:S(2)}) %collective-permute-start) | collective-permute-done | bytes 3145760 | tf_op jit(solution)/shard_map/ppermute | solution.py:9
  526.5 4.7 broadcast_select_fusion
  (159 shorter events, 82.8 us)
Async XLA Ops:
  9.3 22.4 %all-to-all-start = ((s32[64,1,2]{2,1,0:T(1,128)}), s32[64,1,2]{2,1,0:T(1,128)S(1)}, u32[]{:S(2)}, u32[]{:S(2)}) async-start(s32[64,1,2]{2,1,0:T(1,128)} %bitcast.30), calls=%async_computation | async-start | bytes 65536 | tf_op jit(solution)/shard_map/all_to_all | solution.py:33
  34.1 14.0 %all-to-all-start.2 = ((s32[64,1,6]{2,1,0:T(1,128)}), s32[64,1,6]{2,1,0:T(1,128)S(1)}, u32[]{:S(2)}, u32[]{:S(2)}) async-start(s32[64,1,6]{2,1,0:T(1,128)} %bitcast.26), calls=%async_computation.2 | async-start | bytes 65536 | tf_op jit(solution)/shard_map/all_to_all | solution.py:37
  48.1 11.2 %copy-start.1 = (s32[16,6]{0,1:T(8,128)S(1)}, s32[16,6]{0,1:T(8,128)}, u32[]{:S(2)}) copy-start(s32[16,6]{0,1:T(8,128)} %param.7) | copy-start | bytes 1156
  48.1 286.2 %all-to-all-start.1 = ((bf16[64,1,6,64,256]{4,3,2,1,0:T(8,128)(2,1)}), bf16[64,1,6,64,256]{4,3,2,1,0:T(8,128)(2,1)}, u32[]{:S(2)}, u32[]{:S(2)}) async-start(bf16[64,1,6,64,256]{4,3,2,1,0:T(8,128)(2,1)} %bitcast.80), calls=%async_computation.1 | async-start | bytes 25165824 | tf_op jit(solution)/shard_map/all_to_all | solution.py:36
  58.6 1.9 copy-start
  58.6 283.9 %all-gather.2.cloned.1.call-start = ((), (), s32[]{:S(2)}) async-start(), calls=%async_computation.3 | async-start | bytes 15728640 | tf_op jit(solution)/shard_map/all_gather | solution.py:69
  67.7 14.5 %copy-start.2 = (s32[16,6]{0,1:T(8,128)S(1)}, s32[16,6]{0,1:T(8,128)}, u32[]{:S(2)}) copy-start(s32[16,6]{0,1:T(8,128)} %param.8) | copy-start | bytes 1156
  456.8 69.7 %collective-permute-start = (bf16[16,6,64,256]{3,2,1,0:T(8,128)(2,1)S(1)}, bf16[16,6,64,256]{3,2,1,0:T(8,128)(2,1)S(1)}, u32[]{:S(2)}, u32[]{:S(2)}) collective-permute-start(bf16[16,6,64,256]{3,2,1,0:T(8,128)(2,1)S(1)} %divide_convert_fusion), channel_id=1, source_target_pairs={{0,128},{4,132},{8,136},{12,140},{16,144},{20,148},{24,152},{28,15... | collective-permute-start | bytes 9437192 | tf_op jit(solution)/shard_map/ppermute | solution.py:9
Sparse Core Ops, SparseCore 0:
  61.3 122.0 all-gather.1
where the time goes:
time: 542 us; the launch traced here: 538 us
  waiting for transfers between devices  327 us (60%)
  matrix products  71.5 us (13%)
  local copies, waits for them, and re-layouts  61.9 us (11%)
  starting transfers between devices  31.6 us (6%)
  other arithmetic  18.6 us (3%)
  between operations  14.2 us (3%)
  blocking collectives  13.1 us (2%)
    all_to_all x1, waiting for transfers between devices, local(): lax.all_to_all(tiles[asked_slot], 'col', split_axis=0, concat_axis=0, til...  251 us
    ppermute x1, waiting for transfers between devices, shifted(): lax.ppermute(shard, axis, [(i, (i + by) % size) for i in range(size)])  66 us
    dot_general x16, matrix products, one_column(): jnp.einsum('qsrk,skc->qrc', picked, own_piece, preferred_element_type=jnp...  37.9 us
    dot_general x16, matrix products, one_column(): jnp.einsum('qst,strk->qsrk', near_match, near_here, preferred_element_typ...  27.4 us
    gather x2, local copies, waits for them, and re-layouts, local(): near_tiles = tiles[near_slot]  21.7 us
    dynamic_slice x16, local copies, waits for them, and re-layouts, local(): lax.map(one_column, (near_tiles, near_rows, far_tiles, far_rows, tile_row...  16.5 us
    all_to_all x1, starting transfers between devices, local(): lax.all_to_all(request_table, 'col', split_axis=0, concat_axis=0, tiled=T...  13.2 us
    psum x1, blocking collectives, local(): column_sum = lax.psum(local_sums, 'row')  13.1 us
  transfers between devices with their start and end apart: 5, of which 4 were waited for; matrix products, arithmetic and copies ran while one was open for 8% of the time, Pallas kernels for 0%

commit v1 on v0

v1 whole, which is shorter than its diff:
```python
import functools

import jax
import jax.numpy as jnp
from jax import lax
from jax.experimental import pallas as pl
from jax.experimental.pallas import tpu as pltpu
from jax.sharding import PartitionSpec as P

MESH = pl.DeviceIdType.MESH
NEAR = 4
STRIDE = 27
LEVELS = 32767.0


def coded(e):
    top = jnp.maximum(jnp.max(e, axis=0, keepdims=True), 1e-30)
    code = (e * (LEVELS / top) + 0.5).astype(jnp.int32).astype(jnp.int16)
    step = top * (1.0 / LEVELS)
    return code, step * step


def squared(code):
    value = code.astype(jnp.int32).astype(jnp.float32)
    return value * value


def kernel(
    n,
    rows_ref,
    keep_ref,
    hand_ref,
    slot_ref,
    tiles_ref,
    out_ref,
    full,
    stage,
    arrived_a,
    arrived_b,
    acc,
    sums,
    sums_in,
    steps,
    factors,
    factors_in,
    early,
    early_in,
    late,
    late_in,
    x_send,
    x_recv,
    z_send,
    z_recv,
    s_send,
    s_recv,
    h_send,
    h_recv,
):
    count, slots, height, width = tiles_ref.shape
    arrived = (arrived_a, arrived_b)
    half = count // 2
    part = height // 2
    me = lax.axis_index("col")
    x = lax.axis_index("row")
    up, down, across = lax.rem(x + 1, 4), lax.rem(x + 3, 4), lax.rem(x + 2, 4)
    partner = lax.rem(me + n // 2, n)
    mixed = (0,) + tuple(range(NEAR, slots))
    lag = 2
    ahead = 4
    pairs = count // 2
    groups = count // NEAR
    per = 2 * n // pairs

    barrier = pltpu.get_barrier_semaphore()
    for peer in (up, down, across):
        pl.semaphore_signal(barrier, inc=1, device_id={"row": peer}, device_id_type=MESH)

    @pl.loop(1, n)
    def _(t):
        pl.semaphore_signal(
            barrier, inc=1, device_id={"col": lax.rem(me + t, n)}, device_id_type=MESH
        )

    sums[...] = jnp.zeros_like(sums)
    factors[...] = jnp.zeros_like(factors)
    pl.semaphore_wait(barrier, n + 2)

    def direct(j, way):
        return pltpu.make_async_remote_copy(
            src_ref=tiles_ref.at[j],
            dst_ref=full.at[j, x],
            send_sem=x_send.at[way, j],
            recv_sem=x_recv.at[way, j],
            device_id={"row": (up, down)[way]},
            device_id_type=MESH,
        )

    def relay(j, way):
        origin = (down, up)[way]
        return pltpu.make_async_remote_copy(
            src_ref=full.at[j, origin],
            dst_ref=full.at[j, origin],
            send_sem=x_send.at[2, j],
            recv_sem=x_recv.at[2, j],
            device_id={"row": (up, down)[way]},
            device_id_type=MESH,
        )

    def far(h, t):
        return pltpu.make_async_remote_copy(
            src_ref=stage.at[h, t - 1],
            dst_ref=arrived[h].at[t - 1],
            send_sem=z_send.at[h, t - 1],
            recv_sem=z_recv.at[h, t - 1],
            device_id={"col": lax.rem(me + t, n)},
            device_id_type=MESH,
        )

    def total(g, k):
        return pltpu.make_async_remote_copy(
            src_ref=sums.at[g],
            dst_ref=sums_in.at[k, g],
            send_sem=s_send.at[g, k],
            recv_sem=s_recv.at[g, k],
            device_id={"row": (up, down, across)[k]},
            device_id_type=MESH,
        )

    def to_partner(source, target, kind, i):
        return pltpu.make_async_remote_copy(
            src_ref=source,
            dst_ref=target,
            send_sem=h_send.at[kind, i],
            recv_sem=h_recv.at[kind, i],
            device_id={"col": partner},
            device_id_type=MESH,
        )

    def hand_late(h, j):
        return to_partner(late.at[h, j - half], late_in.at[h, j - half], h, j - half)

    def hand_early(j):
        return to_partner(early.at[j - half], early_in.at[j - half], 2, j - half)

    def hand_factor(j):
        return to_partner(factors.at[j - half], factors_in.at[j - half], 3, j - half)

    def send_far(number):
        i = lax.rem(number, n)
        t = lax.rem(i * STRIDE, n)
        pick = slot_ref[t]
        column = lax.rem(pick, count)
        for h in range(2):

            @pl.when((i > 0) & (number // n == h))
            def _():
                rows = pl.ds(h * part, part)
                stage[h, t - 1, 0] = tiles_ref[column, 0, rows]
                stage[h, t - 1, 1] = tiles_ref[column, NEAR + pick // count, rows]
                far(h, t).start()

    @pl.loop(0, lag)
    def _(p):
        for k in range(2):
            for way in range(2):
                direct(count - 1 - k - 2 * p, way).start()

                @pl.loop(0, per // 4)
                def _(m):
                    send_far(p * per + (2 * k + way) * (per // 4) + m)

    @pl.loop(lag * per, ahead * per)
    def _(number):
        send_far(number)

    @pl.loop(0, count)
    def _(j):
        full[j, x] = tiles_ref[j]

    def right(j, s):
        return full[j, :, s].reshape(4 * height, width)

    def row_of(ref, j):
        return ref[j // NEAR, pl.ds(lax.rem(j, NEAR), 1), :]

    def set_row(ref, j, value):
        ref[j // NEAR, pl.ds(lax.rem(j, NEAR), 1), :] = value

    def near(j, hands):
        left = []
        for s in range(NEAR):
            column = j if s == 0 else lax.rem(rows_ref[s, j], count)
            left.append(
                jnp.concatenate([tiles_ref[column, q ^ s] for q in range(NEAR)], axis=0)
            )
        a = jnp.concatenate(left, axis=1)
        b = jnp.concatenate([right(j, s) for s in range(NEAR)], axis=0)
        p = jnp.dot(a, b, preferred_element_type=jnp.float32).reshape(NEAR, height, width)
        acc[j, 0] = p[0]
        column_sum = jnp.zeros((1, width), jnp.float32)
        for q in range(1, NEAR):
            e = p[q] * keep_ref[q, j].astype(jnp.float32)
            if hands:
                early[j - half, q - 1], step = coded(e)
                steps[j - half, q - 1 : q, :] = step
            e = e * e
            acc[j, q] = e
            column_sum = column_sum + jnp.sum(e, axis=0, keepdims=True)
        set_row(sums, j, column_sum)
        c = tiles_ref[j, NEAR:].reshape((slots - NEAR) * height, width)
        acc[j, NEAR:] = jnp.dot(c, right(j, 0), preferred_element_type=jnp.float32).reshape(
            slots - NEAR, height, width
        )
        if hands:
            hand_early(j).start()

    def expand(h, columns, hands):
        rows = pl.ds(h * part, part)
        products = []
        for j in columns:
            for s in range(NEAR, slots):
                t = lax.rem(me - rows_ref[s, j] // count + n, n)
                a = arrived[h][jnp.maximum(t - 1, 0)].reshape(2 * part, width)
                products.append(
                    jnp.dot(a, right(j, s), preferred_element_type=jnp.float32)
                )
        for c, j in enumerate(columns):
            mine = products[c * (slots - NEAR) : (c + 1) * (slots - NEAR)]
            own = acc[j, 0, rows]
            for p in mine:
                own = own + p[part:]
            values = [own] + [acc[j, NEAR + i, rows] + p[:part] for i, p in enumerate(mine)]
            column_sum = row_of(sums, j)
            for i, q in enumerate(mixed):
                e = values[i] * keep_ref[q, j].astype(jnp.float32)
                if hands:
                    late[h, j - half, i], step = coded(e)
                    r = NEAR - 1 + h * len(mixed) + i
                    steps[j - half, r : r + 1, :] = step
                e = e * e
                acc[j, q, rows] = e
                column_sum = column_sum + jnp.sum(e, axis=0, keepdims=True)
            set_row(sums, j, column_sum)
            if hands:
                hand_late(h, j).start()

    def scale_of(j):
        whole = row_of(sums, j)
        for k in range(3):
            whole = whole + row_of(sums_in.at[k], j)
        return width / whole

    def pass_on(p):
        for k in range(2):
            j = count - 1 - k - 2 * p
            direct(j, k).wait_recv()
            relay(j, k).start()
            for way in range(2):

                @pl.when(p + lag < pairs)
                def _():
                    direct(j - 2 * lag, way).start()

                @pl.loop(0, per // 4)
                def _(m):
                    send_far((p + ahead) * per + (2 * k + way) * (per // 4) + m)

    def near_pair(p, hands):
        for k in range(2):
            j = count - 1 - k - 2 * p
            direct(j, 1 - k).wait_recv()
            relay(j, k).wait_recv()
            near(j, hands)

    def await_far(h):
        @pl.loop(1, n)
        def _(t):
            far(h, t).wait_recv()

    def expand_all(h, first, last, hands):
        @pl.loop(0, (last - first) // 2)
        def _(i):
            j = last - 1 - 2 * i
            expand(h, (j, j - 1), hands)

    def start_totals(g):
        for k in range(3):
            total(g, k).start()

    def await_totals(g):
        for k in range(3):
            total(g, k).wait_recv()

    def normalize(g):
        await_totals(g)

        @pl.loop(g * NEAR, (g + 1) * NEAR)
        def _(j):
            scale = scale_of(j)
            for q in range(slots):
                out_ref[j, q] = (acc[j, q] * scale).astype(jnp.bfloat16)

    @pl.loop(0, lag)
    def _(p):
        pass_on(p)

    @pl.loop(lag, pairs // 2 + lag)
    def _(p):
        pass_on(p)
        near_pair(p - lag, True)

    pass_on(pairs // 2 + lag)
    await_far(0)
    expand_all(0, half, count, True)
    near_pair(pairs // 2, False)
    pass_on(pairs // 2 + lag + 1)
    near_pair(pairs // 2 + 1, False)
    expand_all(0, NEAR, 2 * NEAR, False)

    await_far(1)
    for g in (3, 2, 1):
        expand_all(1, g * NEAR, (g + 1) * NEAR, g > 1)
        start_totals(g)

    for g in (3, 2):
        await_totals(g)

        @pl.loop(g * NEAR, (g + 1) * NEAR)
        def _(j):
            scale = scale_of(j)
            for r in range(NEAR - 1 + 2 * len(mixed)):
                factors[j - half, r : r + 1, :] = steps[j - half, r : r + 1, :] * scale
            hand_factor(j).start()

    @pl.loop(pairs // 2 + 2, pairs)
    def _(p):
        near_pair(p, False)

    expand_all(0, 0, NEAR, False)
    expand_all(1, 0, NEAR, False)
    start_totals(0)
    normalize(1)

    first = count - hand_ref[0]

    @pl.loop(0, half)
    def _(i):
        j = count - 1 - i
        hand_factor(j).wait_recv()
        hand_early(j).wait_recv()
        for h in range(2):
            hand_late(h, j).wait_recv()
        scale = scale_of(j)
        take = jnp.full((height, width), j, jnp.int32) >= first
        for q in range(1, NEAR):
            theirs = squared(early_in[j - half, q - 1]) * factors_in[j - half, q - 1 : q, :]
            out_ref[j, q] = jnp.where(take, theirs, acc[j, q] * scale).astype(jnp.bfloat16)
        for i, q in enumerate(mixed):
            for h in range(2):
                rows = pl.ds(h * part, part)
                r = NEAR - 1 + h * len(mixed) + i
                theirs = squared(late_in[h, j - half, i]) * factors_in[j - half, r : r + 1, :]
                out_ref[j, q, rows] = jnp.where(
                    take[:part], theirs, acc[j, q, rows] * scale
                ).astype(jnp.bfloat16)

    normalize(0)

    @pl.loop(0, count)
    def _(j):
        for way in range(2):
            direct(j, way).wait_send()

    @pl.loop(0, pairs)
    def _(p):
        for k in range(2):
            relay(count - 1 - k - 2 * p, k).wait_send()

    @pl.loop(1, n)
    def _(t):
        for h in range(2):
            far(h, t).wait_send()

    @pl.loop(half, count)
    def _(j):
        hand_early(j).wait_send()
        hand_factor(j).wait_send()
        for h in range(2):
            hand_late(h, j).wait_send()

    for g in range(groups):
        for k in range(3):
            total(g, k).wait_send()


def local(n, tiles, tile_rows, keep, hand):
    count, slots, height, width = tiles.shape
    half = count // 2
    part = height // 2
    groups = count // NEAR
    far_count = slots - NEAR
    me = lax.axis_index("col")
    tile_rows = tile_rows.T
    owner = tile_rows[NEAR:] // count
    shift = (owner - me + n) % n
    request = jnp.arange(far_count * count, dtype=jnp.int32).reshape(far_count, count)
    turn = jnp.arange(n, dtype=jnp.int32)[:, None, None]
    slot = jnp.sum(jnp.where(shift[None] == turn, request[None], 0), (1, 2))
    smem = pl.BlockSpec(memory_space=pltpu.SMEM)
    vmem = pl.BlockSpec(memory_space=pltpu.VMEM)
    dma = pltpu.SemaphoreType.DMA
    return pl.pallas_call(
        functools.partial(kernel, n),
        out_shape=pltpu.VMEM(tiles.shape, tiles.dtype),
        in_specs=[smem, smem, smem, smem, vmem],
        out_specs=vmem,
        scratch_shapes=[
            pltpu.VMEM((count, 4, slots, height, width), jnp.bfloat16),
            pltpu.VMEM((2, n - 1, 2, part, width), jnp.bfloat16),
            pltpu.VMEM((n - 1, 2, part, width), jnp.bfloat16),
            pltpu.VMEM((n - 1, 2, part, width), jnp.bfloat16),
            pltpu.VMEM((count, slots, height, width), jnp.float32),
            pltpu.VMEM((groups, 8, width), jnp.float32),
            pltpu.VMEM((3, groups, 8, width), jnp.float32),
            pltpu.VMEM((half, 16, width), jnp.float32),
            pltpu.VMEM((half, 16, width), jnp.float32),
            pltpu.VMEM((half, 16, width), jnp.float32),
            pltpu.VMEM((half, NEAR - 1, height, width), jnp.int16),
            pltpu.VMEM((half, NEAR - 1, height, width), jnp.int16),
            pltpu.VMEM((2, half, 1 + far_count, part, width), jnp.int16),
            pltpu.VMEM((2, half, 1 + far_count, part, width), jnp.int16),
            dma((3, count)),
            dma((3, count)),
            dma((2, n - 1)),
            dma((2, n - 1)),
            dma((groups, 3)),
            dma((groups, 3)),
            dma((4, half)),
            dma((4, half)),
        ],
        compiler_params=pltpu.CompilerParams(
            collective_id=0, has_side_effects=True, vmem_limit_bytes=56 * 1024 * 1024
        ),
        cost_estimate=pl.CostEstimate(
            flops=22 * 2 * count * height * 4 * height * width,
            bytes_accessed=2 * tiles.size * 2,
            transcendentals=0,
        ),
    )(tile_rows, keep.T, hand, slot, tiles)


def solution(mesh):
    placed = (P("col", None, "row", None), P("col", None), P("col", None), P("col"))
    return jax.shard_map(
        functools.partial(local, mesh.shape["col"]),
        mesh=mesh,
        in_specs=placed,
        out_specs=P("col", None, "row", None),
        check_vma=False,
    )
```

time: 542 us -> 132 us (0.24)
  waiting for transfers between devices: 327 us -> 0 us
  Pallas kernels: 0 us -> 129 us
  matrix products: 71.5 us -> 0 us
  local copies, waits for them, and re-layouts: 61.9 us -> 1.67 us
  starting transfers between devices: 31.6 us -> 0 us
  other arithmetic: 18.6 us -> 1.31 us
  between operations: 14.2 us -> 0.66 us
  blocking collectives: 13.1 us -> 0 us
    all_to_all x3 -> x0, waiting for transfers between devices: 260 us -> none  [the longest x1 251 us: local(): lax.all_to_all(tiles[asked_slot], 'col', split_axis=0, concat_axis=0, til...]
    pallas_call x0 -> x1, Pallas kernels: none -> 129 us  [local(): pl.pallas_call(functools.partial(kernel, n), out_shape=pltpu.VMEM(tiles.s...]
    dot_general x48 -> x0, matrix products: 71.5 us -> none  [the longest x16 37.9 us: one_column(): jnp.einsum('qsrk,skc->qrc', picked, own_piece, preferred_element_type=jnp...]
    ppermute x1 -> x0, waiting for transfers between devices: 66 us -> none  [shifted(): lax.ppermute(shard, axis, [(i, (i + by) % size) for i in range(size)])]
    gather x7 -> x0, local copies, waits for them, and re-layouts: 41.4 us -> none  [the longest x2 21.7 us: local(): near_tiles = tiles[near_slot]]
    all_to_all x3 -> x0, starting transfers between devices: 28.3 us -> none  [the longest x1 13.2 us: local(): lax.all_to_all(request_table, 'col', split_axis=0, concat_axis=0, tiled=T...]
    dynamic_slice x16 -> x0, local copies, waits for them, and re-layouts: 16.5 us -> none  [local(): lax.map(one_column, (near_tiles, near_rows, far_tiles, far_rows, tile_row...]
    psum x1 -> x0, blocking collectives: 13.1 us -> none  [local(): column_sum = lax.psum(local_sums, 'row')]
  transfers between devices with their start and end apart: 5 -> 0, of which waited for: 4 -> 0; matrix products, arithmetic and copies ran while one was open for 8% -> 0% of each run, Pallas kernels for 0% -> 0%
where the time goes in v1:
time: 132 us
  Pallas kernels  129 us (98%)
  local copies, waits for them, and re-layouts  1.67 us (1%)
    pallas_call x1, Pallas kernels, local(): pl.pallas_call(functools.partial(kernel, n), out_shape=pltpu.VMEM(tiles.s...  129 us

profile of v1, /device:TPU:1, one launch (start us, length us, event | category | flops | bytes accessed | tf_op | source)
XLA Modules:
  0.0 132.2 jit_solution(1214454062181242199)
XLA Ops:
  0.7 0.7 and_select_fusion
  1.4 0.6 select_reduce_fusion.slot_ref
  2.0 128.5 %shard_map.46 = bf16[16,6,64,256]{3,2,1,0:T(8,128)(2,1)S(1)} custom-call(s32[6,16]{1,0:T(8,128)} %bitcast.3, s32[6,16]{1,0:T(8,128)} %bitcast.4, s32[1]{0:T(128)S(6)} %copy.7.hand_ref, s32[64]{0:T(128)} %select_reduce_fusion.slot_ref, bf16[16,6,64,256]{3,2,1,0:T(8,128)(2,1)} %tiles_ref.1), custom_call_target="tpu_custom_call" | custom-call | flops 2952790016 | bytes 6291456 | tf_op jit(solution)/shard_map/pallas_call | solution.py:412
  130.5 1.7 %copy.6 = bf16[16,6,64,256]{3,2,1,0:T(8,128)(2,1)} copy(bf16[16,6,64,256]{3,2,1,0:T(8,128)(2,1)S(1)} %shard_map.46) | data formatting | bytes 6291456

commit v2 on v1

--- a/solution.py
+++ b/solution.py
@@ -31,8 +31,9 @@
     keep_ref,
     hand_ref,
     slot_ref,
+    source_ref,
+    out_ref,
     tiles_ref,
-    out_ref,
     full,
     stage,
     arrived_a,
@@ -55,6 +56,7 @@
     s_recv,
     h_send,
     h_recv,
+    own_sem,
 ):
     count, slots, height, width = tiles_ref.shape
     arrived = (arrived_a, arrived_b)
@@ -66,10 +68,15 @@
     partner = lax.rem(me + n // 2, n)
     mixed = (0,) + tuple(range(NEAR, slots))
     lag = 2
-    ahead = 4
+    ahead = 2
     pairs = count // 2
     groups = count // NEAR
     per = 2 * n // pairs
+
+    held = pltpu.make_async_copy(source_ref, tiles_ref, own_sem.at[0])
+    held.start()
+    placed = pltpu.make_async_copy(source_ref, full.at[:, x], own_sem.at[1])
+    placed.start()
 
     barrier = pltpu.get_barrier_semaphore()
     for peer in (up, down, across):
@@ -83,6 +90,7 @@
 
     sums[...] = jnp.zeros_like(sums)
     factors[...] = jnp.zeros_like(factors)
+    held.wait()
     pl.semaphore_wait(barrier, n + 2)
 
     def direct(j, way):
@@ -173,9 +181,7 @@
     def _(number):
         send_far(number)
 
-    @pl.loop(0, count)
-    def _(j):
-        full[j, x] = tiles_ref[j]
+    placed.wait()
 
     def right(j, s):
         return full[j, :, s].reshape(4 * height, width)
@@ -412,9 +418,10 @@
     return pl.pallas_call(
         functools.partial(kernel, n),
         out_shape=pltpu.VMEM(tiles.shape, tiles.dtype),
-        in_specs=[smem, smem, smem, smem, vmem],
+        in_specs=[smem, smem, smem, smem, pl.BlockSpec(memory_space=pl.ANY)],
         out_specs=vmem,
         scratch_shapes=[
+            pltpu.VMEM(tiles.shape, tiles.dtype),
             pltpu.VMEM((count, 4, slots, height, width), jnp.bfloat16),
             pltpu.VMEM((2, n - 1, 2, part, width), jnp.bfloat16),
             pltpu.VMEM((n - 1, 2, part, width), jnp.bfloat16),
@@ -437,6 +444,7 @@
             dma((groups, 3)),
             dma((4, half)),
             dma((4, half)),
+            dma((2,)),
         ],
         compiler_params=pltpu.CompilerParams(
             collective_id=0, has_side_effects=True, vmem_limit_bytes=56 * 1024 * 1024

time: 132 us -> 131 us (level)
  Pallas kernels: 129 us -> 127 us
where the time goes in v2:
time: 131 us
  Pallas kernels  127 us (97%)
  local copies, waits for them, and re-layouts  1.67 us (1%)
  other arithmetic  1.31 us (1%)
    pallas_call x1, Pallas kernels, local(): pl.pallas_call(functools.partial(kernel, n), out_shape=pltpu.VMEM(tiles.s...  127 us

profile of v2, /device:TPU:1, one launch (start us, length us, event | category | flops | bytes accessed | tf_op | source)
XLA Modules:
  0.0 131.1 jit_solution(15460729615204779004)
XLA Ops:
  0.7 0.7 and_select_fusion
  1.4 0.6 select_reduce_fusion.slot_ref
  2.0 127.4 %shard_map.46 = bf16[16,6,64,256]{3,2,1,0:T(8,128)(2,1)S(1)} custom-call(s32[6,16]{1,0:T(8,128)} %bitcast.3, s32[6,16]{1,0:T(8,128)} %bitcast.4, s32[1]{0:T(128)S(6)} %copy.7.hand_ref, s32[64]{0:T(128)} %select_reduce_fusion.slot_ref, bf16[16,6,64,256]{3,2,1,0:T(8,128)(2,1)} %source_ref.1), custom_call_target="tpu_custom_call" | custom-call | flops 2952790016 | bytes 6291456 | tf_op jit(solution)/shard_map/pallas_call | solution.py:418
  129.4 1.7 %copy.6 = bf16[16,6,64,256]{3,2,1,0:T(8,128)(2,1)} copy(bf16[16,6,64,256]{3,2,1,0:T(8,128)(2,1)S(1)} %shard_map.46) | data formatting | bytes 6291456

commit v3 on v2

--- a/solution.py
+++ b/solution.py
@@ -97,7 +97,7 @@
         return pltpu.make_async_remote_copy(
             src_ref=tiles_ref.at[j],
             dst_ref=full.at[j, x],
-            send_sem=x_send.at[way, j],
+            send_sem=x_send.at[way],
             recv_sem=x_recv.at[way, j],
             device_id={"row": (up, down)[way]},
             device_id_type=MESH,
@@ -108,7 +108,7 @@
         return pltpu.make_async_remote_copy(
             src_ref=full.at[j, origin],
             dst_ref=full.at[j, origin],
-            send_sem=x_send.at[2, j],
+            send_sem=x_send.at[2],
             recv_sem=x_recv.at[2, j],
             device_id={"row": (up, down)[way]},
             device_id_type=MESH,
@@ -118,9 +118,29 @@
         return pltpu.make_async_remote_copy(
             src_ref=stage.at[h, t - 1],
             dst_ref=arrived[h].at[t - 1],
-            send_sem=z_send.at[h, t - 1],
-            recv_sem=z_recv.at[h, t - 1],
+            send_sem=z_send.at[h],
+            recv_sem=z_recv.at[h],
             device_id={"col": lax.rem(me + t, n)},
+            device_id_type=MESH,
+        )
+
+    def all_far(h):
+        return pltpu.make_async_remote_copy(
+            src_ref=stage.at[h],
+            dst_ref=arrived[h],
+            send_sem=z_send.at[h],
+            recv_sem=z_recv.at[h],
+            device_id={"col": partner},
+            device_id_type=MESH,
+        )
+
+    def all_rows(way):
+        return pltpu.make_async_remote_copy(
+            src_ref=tiles_ref,
+            dst_ref=full.at[:, x],
+            send_sem=x_send.at[way],
+            recv_sem=x_recv.at[0, 0],
+            device_id={"row": up},
             device_id_type=MESH,
         )
 
@@ -128,7 +148,7 @@
         return pltpu.make_async_remote_copy(
             src_ref=sums.at[g],
             dst_ref=sums_in.at[k, g],
-            send_sem=s_send.at[g, k],
+            send_sem=s_send.at[k],
             recv_sem=s_recv.at[g, k],
             device_id={"row": (up, down, across)[k]},
             device_id_type=MESH,
@@ -138,7 +158,7 @@
         return pltpu.make_async_remote_copy(
             src_ref=source,
             dst_ref=target,
-            send_sem=h_send.at[kind, i],
+            send_sem=h_send.at[kind],
             recv_sem=h_recv.at[kind, i],
             device_id={"col": partner},
             device_id_type=MESH,
@@ -279,9 +299,7 @@
             near(j, hands)
 
     def await_far(h):
-        @pl.loop(1, n)
-        def _(t):
-            far(h, t).wait_recv()
+        all_far(h).wait_recv()
 
     def expand_all(h, first, last, hands):
         @pl.loop(0, (last - first) // 2)
@@ -372,31 +390,22 @@
 
     normalize(0)
 
-    @pl.loop(0, count)
-    def _(j):
-        for way in range(2):
-            direct(j, way).wait_send()
-
-    @pl.loop(0, pairs)
-    def _(p):
-        for k in range(2):
-            relay(count - 1 - k - 2 * p, k).wait_send()
-
-    @pl.loop(1, n)
-    def _(t):
-        for h in range(2):
-            far(h, t).wait_send()
-
-    @pl.loop(half, count)
-    def _(j):
-        hand_early(j).wait_send()
-        hand_factor(j).wait_send()
-        for h in range(2):
-            hand_late(h, j).wait_send()
-
-    for g in range(groups):
-        for k in range(3):
-            total(g, k).wait_send()
+    for way in range(3):
+        all_rows(way).wait_send()
+    for h in range(2):
+        all_far(h).wait_send()
+        to_partner(late.at[h], late_in.at[h], h, 0).wait_send()
+    to_partner(early, early_in, 2, 0).wait_send()
+    to_partner(factors, factors_in, 3, 0).wait_send()
+    for k in range(3):
+        pltpu.make_async_remote_copy(
+            src_ref=sums,
+            dst_ref=sums_in.at[k],
+            send_sem=s_send.at[k],
+            recv_sem=s_recv.at[0, k],
+            device_id={"row": up},
+            device_id_type=MESH,
+        ).wait_send()
 
 
 def local(n, tiles, tile_rows, keep, hand):
@@ -436,13 +445,13 @@
             pltpu.VMEM((half, NEAR - 1, height, width), jnp.int16),
             pltpu.VMEM((2, half, 1 + far_count, part, width), jnp.int16),
             pltpu.VMEM((2, half, 1 + far_count, part, width), jnp.int16),
+            dma((3,)),
             dma((3, count)),
-            dma((3, count)),
-            dma((2, n - 1)),
-            dma((2, n - 1)),
+            dma((2,)),
+            dma((2,)),
+            dma((3,)),
             dma((groups, 3)),
-            dma((groups, 3)),
-            dma((4, half)),
+            dma((4,)),
             dma((4, half)),
             dma((2,)),
         ],

time: 131 us -> 127 us (0.969)
  Pallas kernels: 127 us -> 124 us
    pallas_call x1, Pallas kernels: 127 us -> 124 us  [local(): pl.pallas_call(functools.partial(kernel, n), out_shape=pltpu.VMEM(tiles.s...]
where the time goes in v3:
time: 127 us
  Pallas kernels  124 us (98%)
  local copies, waits for them, and re-layouts  1.67 us (1%)
  other arithmetic  1.31 us (1%)
    pallas_call x1, Pallas kernels, local(): pl.pallas_call(functools.partial(kernel, n), out_shape=pltpu.VMEM(tiles.s...  124 us

profile of v3, /device:TPU:1, one launch (start us, length us, event | category | flops | bytes accessed | tf_op | source)
XLA Modules:
  0.0 127.3 jit_solution(8513218368025938563)
XLA Ops:
  0.7 0.7 and_select_fusion
  1.4 0.6 select_reduce_fusion.slot_ref
  2.0 123.6 %shard_map.46 = bf16[16,6,64,256]{3,2,1,0:T(8,128)(2,1)S(1)} custom-call(s32[6,16]{1,0:T(8,128)} %bitcast.3, s32[6,16]{1,0:T(8,128)} %bitcast.4, s32[1]{0:T(128)S(6)} %copy.7.hand_ref, s32[64]{0:T(128)} %select_reduce_fusion.slot_ref, bf16[16,6,64,256]{3,2,1,0:T(8,128)(2,1)} %source_ref.1), custom_call_target="tpu_custom_call" | custom-call | flops 2952790016 | bytes 6291456 | tf_op jit(solution)/shard_map/pallas_call | solution.py:427
  125.6 1.7 %copy.6 = bf16[16,6,64,256]{3,2,1,0:T(8,128)(2,1)} copy(bf16[16,6,64,256]{3,2,1,0:T(8,128)(2,1)S(1)} %shard_map.46) | data formatting | bytes 6291456

commit v4 on v3

--- a/solution.py
+++ b/solution.py
@@ -241,21 +241,23 @@
             hand_early(j).start()
 
     def expand(h, columns, hands):
-        rows = pl.ds(h * part, part)
+        halves = (0, 1) if h is None else (h,)
+        rows = pl.ds(halves[0] * part, len(halves) * part)
         products = []
         for j in columns:
             for s in range(NEAR, slots):
                 t = lax.rem(me - rows_ref[s, j] // count + n, n)
-                a = arrived[h][jnp.maximum(t - 1, 0)].reshape(2 * part, width)
-                products.append(
-                    jnp.dot(a, right(j, s), preferred_element_type=jnp.float32)
+                a = jnp.concatenate(
+                    [arrived[i][jnp.maximum(t - 1, 0), k] for k in range(2) for i in halves], axis=0
                 )
+                products.append(jnp.dot(a, right(j, s), preferred_element_type=jnp.float32))
+        edge = len(halves) * part
         for c, j in enumerate(columns):
             mine = products[c * (slots - NEAR) : (c + 1) * (slots - NEAR)]
             own = acc[j, 0, rows]
             for p in mine:
-                own = own + p[part:]
-            values = [own] + [acc[j, NEAR + i, rows] + p[:part] for i, p in enumerate(mine)]
+                own = own + p[edge:]
+            values = [own] + [acc[j, NEAR + i, rows] + p[:edge] for i, p in enumerate(mine)]
             column_sum = row_of(sums, j)
             for i, q in enumerate(mixed):
                 e = values[i] * keep_ref[q, j].astype(jnp.float32)
@@ -356,14 +358,12 @@
                 factors[j - half, r : r + 1, :] = steps[j - half, r : r + 1, :] * scale
             hand_factor(j).start()
 
-    @pl.loop(pairs // 2 + 2, pairs)
-    def _(p):
-        near_pair(p, False)
-
-    expand_all(0, 0, NEAR, False)
-    expand_all(1, 0, NEAR, False)
+    near_pair(6, False)
+    expand(None, (3, 2), False)
+    normalize(1)
+    near_pair(7, False)
+    expand(None, (1, 0), False)
     start_totals(0)
-    normalize(1)
 
     first = count - hand_ref[0]
 

time: 127 us -> 127 us (level)
  no operation moved by 1% of the time
where the time goes in v4:
time: 127 us
  Pallas kernels  123 us (97%)
  local copies, waits for them, and re-layouts  1.67 us (1%)
  other arithmetic  1.31 us (1%)
    pallas_call x1, Pallas kernels, local(): pl.pallas_call(functools.partial(kernel, n), out_shape=pltpu.VMEM(tiles.s...  123 us

profile of v4, /device:TPU:1, one launch (start us, length us, event | category | flops | bytes accessed | tf_op | source)
XLA Modules:
  0.0 126.7 jit_solution(9357399804307143965)
XLA Ops:
  0.7 0.7 and_select_fusion
  1.4 0.6 select_reduce_fusion.slot_ref
  2.0 123.0 %shard_map.46 = bf16[16,6,64,256]{3,2,1,0:T(8,128)(2,1)S(1)} custom-call(s32[6,16]{1,0:T(8,128)} %bitcast.3, s32[6,16]{1,0:T(8,128)} %bitcast.4, s32[1]{0:T(128)S(6)} %copy.7.hand_ref, s32[64]{0:T(128)} %select_reduce_fusion.slot_ref, bf16[16,6,64,256]{3,2,1,0:T(8,128)(2,1)} %source_ref.1), custom_call_target="tpu_custom_call" | custom-call | flops 2952790016 | bytes 6291456 | tf_op jit(solution)/shard_map/pallas_call | solution.py:427
  125.0 1.7 %copy.6 = bf16[16,6,64,256]{3,2,1,0:T(8,128)(2,1)} copy(bf16[16,6,64,256]{3,2,1,0:T(8,128)(2,1)S(1)} %shard_map.46) | data formatting | bytes 6291456

commit v5 on v4

--- a/solution.py
+++ b/solution.py
@@ -11,6 +11,7 @@
 NEAR = 4
 STRIDE = 27
 LEVELS = 32767.0
+LAST = 16
 
 
 def coded(e):
@@ -35,7 +36,8 @@
     out_ref,
     tiles_ref,
     full,
-    stage,
+    stage_a,
+    stage_b,
     arrived_a,
     arrived_b,
     acc,
@@ -46,8 +48,10 @@
     factors_in,
     early,
     early_in,
-    late,
-    late_in,
+    late_a,
+    late_b,
+    late_in_a,
+    late_in_b,
     x_send,
     x_recv,
     z_send,
@@ -59,9 +63,10 @@
     own_sem,
 ):
     count, slots, height, width = tiles_ref.shape
-    arrived = (arrived_a, arrived_b)
+    stage, arrived = (stage_a, stage_b), (arrived_a, arrived_b)
+    late, late_in = (late_a, late_b), (late_in_a, late_in_b)
     half = count // 2
-    part = height // 2
+    parts = ((0, height - LAST), (height - LAST, LAST))
     me = lax.axis_index("col")
     x = lax.axis_index("row")
     up, down, across = lax.rem(x + 1, 4), lax.rem(x + 3, 4), lax.rem(x + 2, 4)
@@ -116,7 +121,7 @@
 
     def far(h, t):
         return pltpu.make_async_remote_copy(
-            src_ref=stage.at[h, t - 1],
+            src_ref=stage[h].at[t - 1],
             dst_ref=arrived[h].at[t - 1],
             send_sem=z_send.at[h],
             recv_sem=z_recv.at[h],
@@ -126,7 +131,7 @@
 
     def all_far(h):
         return pltpu.make_async_remote_copy(
-            src_ref=stage.at[h],
+            src_ref=stage[h],
             dst_ref=arrived[h],
             send_sem=z_send.at[h],
             recv_sem=z_recv.at[h],
@@ -165,7 +170,7 @@
         )
 
     def hand_late(h, j):
-        return to_partner(late.at[h, j - half], late_in.at[h, j - half], h, j - half)
+        return to_partner(late[h].at[j - half], late_in[h].at[j - half], h, j - half)
 
     def hand_early(j):
         return to_partner(early.at[j - half], early_in.at[j - half], 2, j - half)
@@ -182,9 +187,9 @@
 
             @pl.when((i > 0) & (number // n == h))
             def _():
-                rows = pl.ds(h * part, part)
-                stage[h, t - 1, 0] = tiles_ref[column, 0, rows]
-                stage[h, t - 1, 1] = tiles_ref[column, NEAR + pick // count, rows]
+                rows = pl.ds(*parts[h])
+                stage[h][t - 1, 0] = tiles_ref[column, 0, rows]
+                stage[h][t - 1, 1] = tiles_ref[column, NEAR + pick // count, rows]
                 far(h, t).start()
 
     @pl.loop(0, lag)
@@ -242,7 +247,8 @@
 
     def expand(h, columns, hands):
         halves = (0, 1) if h is None else (h,)
-        rows = pl.ds(halves[0] * part, len(halves) * part)
+        edge = sum(parts[i][1] for i in halves)
+        rows = pl.ds(parts[halves[0]][0], edge)
         products = []
         for j in columns:
             for s in range(NEAR, slots):
@@ -251,7 +257,6 @@
                     [arrived[i][jnp.maximum(t - 1, 0), k] for k in range(2) for i in halves], axis=0
                 )
                 products.append(jnp.dot(a, right(j, s), preferred_element_type=jnp.float32))
-        edge = len(halves) * part
         for c, j in enumerate(columns):
             mine = products[c * (slots - NEAR) : (c + 1) * (slots - NEAR)]
             own = acc[j, 0, rows]
@@ -262,7 +267,7 @@
             for i, q in enumerate(mixed):
                 e = values[i] * keep_ref[q, j].astype(jnp.float32)
                 if hands:
-                    late[h, j - half, i], step = coded(e)
+                    late[h][j - half, i], step = coded(e)
                     r = NEAR - 1 + h * len(mixed) + i
                     steps[j - half, r : r + 1, :] = step
                 e = e * e
@@ -335,18 +340,18 @@
         pass_on(p)
         near_pair(p - lag, True)
 
-    pass_on(pairs // 2 + lag)
+    pass_on(6)
     await_far(0)
     expand_all(0, half, count, True)
-    near_pair(pairs // 2, False)
-    pass_on(pairs // 2 + lag + 1)
-    near_pair(pairs // 2 + 1, False)
-    expand_all(0, NEAR, 2 * NEAR, False)
-
+    near_pair(4, False)
+    pass_on(7)
     await_far(1)
-    for g in (3, 2, 1):
-        expand_all(1, g * NEAR, (g + 1) * NEAR, g > 1)
+    for g in (3, 2):
+        expand_all(1, g * NEAR, (g + 1) * NEAR, True)
         start_totals(g)
+    near_pair(5, False)
+    expand_all(None, NEAR, 2 * NEAR, False)
+    start_totals(1)
 
     for g in (3, 2):
         await_totals(g)
@@ -381,11 +386,11 @@
             out_ref[j, q] = jnp.where(take, theirs, acc[j, q] * scale).astype(jnp.bfloat16)
         for i, q in enumerate(mixed):
             for h in range(2):
-                rows = pl.ds(h * part, part)
+                rows = pl.ds(*parts[h])
                 r = NEAR - 1 + h * len(mixed) + i
-                theirs = squared(late_in[h, j - half, i]) * factors_in[j - half, r : r + 1, :]
+                theirs = squared(late_in[h][j - half, i]) * factors_in[j - half, r : r + 1, :]
                 out_ref[j, q, rows] = jnp.where(
-                    take[:part], theirs, acc[j, q, rows] * scale
+                    take[: parts[h][1]], theirs, acc[j, q, rows] * scale
                 ).astype(jnp.bfloat16)
 
     normalize(0)
@@ -394,7 +399,7 @@
         all_rows(way).wait_send()
     for h in range(2):
         all_far(h).wait_send()
-        to_partner(late.at[h], late_in.at[h], h, 0).wait_send()
+        to_partner(late[h], late_in[h], h, 0).wait_send()
     to_partner(early, early_in, 2, 0).wait_send()
     to_partner(factors, factors_in, 3, 0).wait_send()
     for k in range(3):
@@ -411,7 +416,6 @@
 def local(n, tiles, tile_rows, keep, hand):
     count, slots, height, width = tiles.shape
     half = count // 2
-    part = height // 2
     groups = count // NEAR
     far_count = slots - NEAR
     me = lax.axis_index("col")
@@ -432,9 +436,10 @@
         scratch_shapes=[
             pltpu.VMEM(tiles.shape, tiles.dtype),
             pltpu.VMEM((count, 4, slots, height, width), jnp.bfloat16),
-            pltpu.VMEM((2, n - 1, 2, part, width), jnp.bfloat16),
-            pltpu.VMEM((n - 1, 2, part, width), jnp.bfloat16),
-            pltpu.VMEM((n - 1, 2, part, width), jnp.bfloat16),
+            pltpu.VMEM((n - 1, 2, height - LAST, width), jnp.bfloat16),
+            pltpu.VMEM((n - 1, 2, LAST, width), jnp.bfloat16),
+            pltpu.VMEM((n - 1, 2, height - LAST, width), jnp.bfloat16),
+            pltpu.VMEM((n - 1, 2, LAST, width), jnp.bfloat16),
             pltpu.VMEM((count, slots, height, width), jnp.float32),
             pltpu.VMEM((groups, 8, width), jnp.float32),
             pltpu.VMEM((3, groups, 8, width), jnp.float32),
@@ -443,8 +448,10 @@
             pltpu.VMEM((half, 16, width), jnp.float32),
             pltpu.VMEM((half, NEAR - 1, height, width), jnp.int16),
             pltpu.VMEM((half, NEAR - 1, height, width), jnp.int16),
-            pltpu.VMEM((2, half, 1 + far_count, part, width), jnp.int16),
-            pltpu.VMEM((2, half, 1 + far_count, part, width), jnp.int16),
+            pltpu.VMEM((half, 1 + far_count, height - LAST, width), jnp.int16),
+            pltpu.VMEM((half, 1 + far_count, LAST, width), jnp.int16),
+            pltpu.VMEM((half, 1 + far_count, height - LAST, width), jnp.int16),
+            pltpu.VMEM((half, 1 + far_count, LAST, width), jnp.int16),
             dma((3,)),
             dma((3, count)),
             dma((2,)),

time: 127 us -> 127 us (level)
  no operation moved by 1% of the time
where the time goes in v5:
time: 127 us
  Pallas kernels  123 us (97%)
  local copies, waits for them, and re-layouts  1.67 us (1%)
  other arithmetic  1.31 us (1%)
    pallas_call x1, Pallas kernels, local(): pl.pallas_call(functools.partial(kernel, n), out_shape=pltpu.VMEM(tiles.s...  123 us

profile of v5, /device:TPU:1, one launch (start us, length us, event | category | flops | bytes accessed | tf_op | source)
XLA Modules:
  0.0 126.7 jit_solution(11077322779524623336)
XLA Ops:
  0.7 0.7 and_select_fusion
  1.4 0.6 select_reduce_fusion.slot_ref
  2.0 123.1 %shard_map.46 = bf16[16,6,64,256]{3,2,1,0:T(8,128)(2,1)S(1)} custom-call(s32[6,16]{1,0:T(8,128)} %bitcast.3, s32[6,16]{1,0:T(8,128)} %bitcast.4, s32[1]{0:T(128)S(6)} %copy.7.hand_ref, s32[64]{0:T(128)} %select_reduce_fusion.slot_ref, bf16[16,6,64,256]{3,2,1,0:T(8,128)(2,1)} %source_ref.1), custom_call_target="tpu_custom_call" | custom-call | flops 2952790016 | bytes 6291456 | tf_op jit(solution)/shard_map/pallas_call | solution.py:431
  125.0 1.7 %copy.6 = bf16[16,6,64,256]{3,2,1,0:T(8,128)(2,1)} copy(bf16[16,6,64,256]{3,2,1,0:T(8,128)(2,1)S(1)} %shard_map.46) | data formatting | bytes 6291456

commit v6 on v5

--- a/solution.py
+++ b/solution.py
@@ -363,36 +363,39 @@
                 factors[j - half, r : r + 1, :] = steps[j - half, r : r + 1, :] * scale
             hand_factor(j).start()
 
+    first = count - hand_ref[0]
+
+    def finish(g):
+        @pl.loop(0, NEAR)
+        def _(i):
+            j = (g + 1) * NEAR - 1 - i
+            hand_factor(j).wait_recv()
+            hand_early(j).wait_recv()
+            for h in range(2):
+                hand_late(h, j).wait_recv()
+            scale = scale_of(j)
+            take = jnp.full((height, width), j, jnp.int32) >= first
+            for q in range(1, NEAR):
+                theirs = squared(early_in[j - half, q - 1]) * factors_in[j - half, q - 1 : q, :]
+                out_ref[j, q] = jnp.where(take, theirs, acc[j, q] * scale).astype(jnp.bfloat16)
+            for i, q in enumerate(mixed):
+                for h in range(2):
+                    rows = pl.ds(*parts[h])
+                    r = NEAR - 1 + h * len(mixed) + i
+                    theirs = squared(late_in[h][j - half, i]) * factors_in[j - half, r : r + 1, :]
+                    out_ref[j, q, rows] = jnp.where(
+                        take[: parts[h][1]], theirs, acc[j, q, rows] * scale
+                    ).astype(jnp.bfloat16)
+
+
     near_pair(6, False)
     expand(None, (3, 2), False)
     normalize(1)
+    finish(3)
     near_pair(7, False)
     expand(None, (1, 0), False)
     start_totals(0)
-
-    first = count - hand_ref[0]
-
-    @pl.loop(0, half)
-    def _(i):
-        j = count - 1 - i
-        hand_factor(j).wait_recv()
-        hand_early(j).wait_recv()
-        for h in range(2):
-            hand_late(h, j).wait_recv()
-        scale = scale_of(j)
-        take = jnp.full((height, width), j, jnp.int32) >= first
-        for q in range(1, NEAR):
-            theirs = squared(early_in[j - half, q - 1]) * factors_in[j - half, q - 1 : q, :]
-            out_ref[j, q] = jnp.where(take, theirs, acc[j, q] * scale).astype(jnp.bfloat16)
-        for i, q in enumerate(mixed):
-            for h in range(2):
-                rows = pl.ds(*parts[h])
-                r = NEAR - 1 + h * len(mixed) + i
-                theirs = squared(late_in[h][j - half, i]) * factors_in[j - half, r : r + 1, :]
-                out_ref[j, q, rows] = jnp.where(
-                    take[: parts[h][1]], theirs, acc[j, q, rows] * scale
-                ).astype(jnp.bfloat16)
-
+    finish(2)
     normalize(0)
 
     for way in range(3):
@@ -420,11 +423,14 @@
     far_count = slots - NEAR
     me = lax.axis_index("col")
     tile_rows = tile_rows.T
-    owner = tile_rows[NEAR:] // count
-    shift = (owner - me + n) % n
-    request = jnp.arange(far_count * count, dtype=jnp.int32).reshape(far_count, count)
-    turn = jnp.arange(n, dtype=jnp.int32)[:, None, None]
-    slot = jnp.sum(jnp.where(shift[None] == turn, request[None], 0), (1, 2))
+    shape = (n, far_count, count)
+    low = lax.broadcasted_iota(jnp.int32, shape, 0) * count
+    request = lax.broadcasted_iota(jnp.int32, shape, 1) * count + lax.broadcasted_iota(
+        jnp.int32, shape, 2
+    )
+    ahead = tile_rows[NEAR:] - me * count
+    ahead = jnp.broadcast_to(jnp.where(ahead < 0, ahead + n * count, ahead)[None], shape)
+    slot = jnp.sum(jnp.where((ahead >= low) & (ahead < low + count), request, 0), (1, 2))
     smem = pl.BlockSpec(memory_space=pltpu.SMEM)
     vmem = pl.BlockSpec(memory_space=pltpu.VMEM)
     dma = pltpu.SemaphoreType.DMA

time: 127 us -> 129 us (1.016)
    pallas_call x1, Pallas kernels: 123 us -> 124 us  [local(): pl.pallas_call(functools.partial(kernel, n), out_shape=pltpu.VMEM(tiles.s...]
where the time goes in v6:
time: 129 us; the launch traced here: 128 us
  Pallas kernels  124 us (96%)
  local copies, waits for them, and re-layouts  1.67 us (1%)
  other arithmetic  1.3 us (1%)
    pallas_call x1, Pallas kernels, local(): pl.pallas_call(functools.partial(kernel, n), out_shape=pltpu.VMEM(tiles.s...  124 us

profile of v6, /device:TPU:1, one launch (start us, length us, event | category | flops | bytes accessed | tf_op | source)
XLA Modules:
  0.0 128.1 jit_solution(11830711998141688120)
XLA Ops:
  0.7 0.7 compare_select_fusion
  1.4 0.6 select_reduce_fusion.slot_ref
  2.0 124.5 %shard_map.46 = bf16[16,6,64,256]{3,2,1,0:T(8,128)(2,1)S(1)} custom-call(s32[6,16]{1,0:T(8,128)} %bitcast.3, s32[6,16]{1,0:T(8,128)} %bitcast.4, s32[1]{0:T(128)S(6)} %copy.7.hand_ref, s32[64]{0:T(128)} %select_reduce_fusion.slot_ref, bf16[16,6,64,256]{3,2,1,0:T(8,128)(2,1)} %source_ref.1), custom_call_target="tpu_custom_call" | custom-call | flops 2952790016 | bytes 6291456 | tf_op jit(solution)/shard_map/pallas_call | solution.py:437
  126.4 1.7 %copy.6 = bf16[16,6,64,256]{3,2,1,0:T(8,128)(2,1)} copy(bf16[16,6,64,256]{3,2,1,0:T(8,128)(2,1)S(1)} %shard_map.46) | data formatting | bytes 6291456
  (2 shorter events, 0.0 us)

commit v7 on v5

--- a/solution.py
+++ b/solution.py
@@ -73,7 +73,7 @@
     partner = lax.rem(me + n // 2, n)
     mixed = (0,) + tuple(range(NEAR, slots))
     lag = 2
-    ahead = 2
+    ahead = 4
     pairs = count // 2
     groups = count // NEAR
     per = 2 * n // pairs
@@ -349,9 +349,6 @@
     for g in (3, 2):
         expand_all(1, g * NEAR, (g + 1) * NEAR, True)
         start_totals(g)
-    near_pair(5, False)
-    expand_all(None, NEAR, 2 * NEAR, False)
-    start_totals(1)
 
     for g in (3, 2):
         await_totals(g)
@@ -362,6 +359,10 @@
             for r in range(NEAR - 1 + 2 * len(mixed)):
                 factors[j - half, r : r + 1, :] = steps[j - half, r : r + 1, :] * scale
             hand_factor(j).start()
+
+    near_pair(5, False)
+    expand_all(None, NEAR, 2 * NEAR, False)
+    start_totals(1)
 
     near_pair(6, False)
     expand(None, (3, 2), False)

time: 127 us -> 131 us (1.031)
  Pallas kernels: 123 us -> 127 us
    pallas_call x1, Pallas kernels: 123 us -> 127 us  [local(): pl.pallas_call(functools.partial(kernel, n), out_shape=pltpu.VMEM(tiles.s...]
where the time goes in v7:
time: 131 us; the launch traced here: 130 us
  Pallas kernels  127 us (97%)
  local copies, waits for them, and re-layouts  1.67 us (1%)
  other arithmetic  1.31 us (1%)
    pallas_call x1, Pallas kernels, local(): pl.pallas_call(functools.partial(kernel, n), out_shape=pltpu.VMEM(tiles.s...  127 us

profile of v7, /device:TPU:1, one launch (start us, length us, event | category | flops | bytes accessed | tf_op | source)
XLA Modules:
  0.0 130.2 jit_solution(7805860583979181915)
XLA Ops:
  0.7 0.7 and_select_fusion
  1.4 0.6 select_reduce_fusion.slot_ref
  2.0 126.6 %shard_map.46 = bf16[16,6,64,256]{3,2,1,0:T(8,128)(2,1)S(1)} custom-call(s32[6,16]{1,0:T(8,128)} %bitcast.3, s32[6,16]{1,0:T(8,128)} %bitcast.4, s32[1]{0:T(128)S(6)} %copy.7.hand_ref, s32[64]{0:T(128)} %select_reduce_fusion.slot_ref, bf16[16,6,64,256]{3,2,1,0:T(8,128)(2,1)} %source_ref.1), custom_call_target="tpu_custom_call" | custom-call | flops 2952790016 | bytes 6291456 | tf_op jit(solution)/shard_map/pallas_call | solution.py:432
  128.6 1.7 %copy.6 = bf16[16,6,64,256]{3,2,1,0:T(8,128)(2,1)} copy(bf16[16,6,64,256]{3,2,1,0:T(8,128)(2,1)S(1)} %shard_map.46) | data formatting | bytes 6291456

commit v8 on v5

--- a/solution.py
+++ b/solution.py
@@ -73,7 +73,7 @@
     partner = lax.rem(me + n // 2, n)
     mixed = (0,) + tuple(range(NEAR, slots))
     lag = 2
-    ahead = 2
+    ahead = 1
     pairs = count // 2
     groups = count // NEAR
     per = 2 * n // pairs
@@ -198,13 +198,11 @@
             for way in range(2):
                 direct(count - 1 - k - 2 * p, way).start()
 
-                @pl.loop(0, per // 4)
-                def _(m):
-                    send_far(p * per + (2 * k + way) * (per // 4) + m)
-
-    @pl.loop(lag * per, ahead * per)
-    def _(number):
-        send_far(number)
+                @pl.when(p < ahead)
+                def _():
+                    @pl.loop(0, per // 4)
+                    def _(m):
+                        send_far(p * per + (2 * k + way) * (per // 4) + m)
 
     placed.wait()
 

time: 127 us -> 127 us (level)
  no operation moved by 1% of the time
where the time goes in v8:
time: 127 us
  Pallas kernels  123 us (97%)
  local copies, waits for them, and re-layouts  1.67 us (1%)
  other arithmetic  1.31 us (1%)
    pallas_call x1, Pallas kernels, local(): pl.pallas_call(functools.partial(kernel, n), out_shape=pltpu.VMEM(tiles.s...  123 us

profile of v8, /device:TPU:1, one launch (start us, length us, event | category | flops | bytes accessed | tf_op | source)
XLA Modules:
  0.0 126.7 jit_solution(1405987480525477870)
XLA Ops:
  0.7 0.7 and_select_fusion
  1.4 0.6 select_reduce_fusion.slot_ref
  2.0 123.1 %shard_map.46 = bf16[16,6,64,256]{3,2,1,0:T(8,128)(2,1)S(1)} custom-call(s32[6,16]{1,0:T(8,128)} %bitcast.3, s32[6,16]{1,0:T(8,128)} %bitcast.4, s32[1]{0:T(128)S(6)} %copy.7.hand_ref, s32[64]{0:T(128)} %select_reduce_fusion.slot_ref, bf16[16,6,64,256]{3,2,1,0:T(8,128)(2,1)} %source_ref.1), custom_call_target="tpu_custom_call" | custom-call | flops 2952790016 | bytes 6291456 | tf_op jit(solution)/shard_map/pallas_call | solution.py:429
  125.0 1.7 %copy.6 = bf16[16,6,64,256]{3,2,1,0:T(8,128)(2,1)} copy(bf16[16,6,64,256]{3,2,1,0:T(8,128)(2,1)S(1)} %shard_map.46) | data formatting | bytes 6291456

commit v9 on v8

--- a/solution.py
+++ b/solution.py
@@ -347,9 +347,6 @@
     for g in (3, 2):
         expand_all(1, g * NEAR, (g + 1) * NEAR, True)
         start_totals(g)
-    near_pair(5, False)
-    expand_all(None, NEAR, 2 * NEAR, False)
-    start_totals(1)
 
     for g in (3, 2):
         await_totals(g)
@@ -360,6 +357,10 @@
             for r in range(NEAR - 1 + 2 * len(mixed)):
                 factors[j - half, r : r + 1, :] = steps[j - half, r : r + 1, :] * scale
             hand_factor(j).start()
+
+    near_pair(5, False)
+    expand_all(None, NEAR, 2 * NEAR, False)
+    start_totals(1)
 
     near_pair(6, False)
     expand(None, (3, 2), False)

time: 127 us -> 131 us (1.031)
  Pallas kernels: 123 us -> 127 us
    pallas_call x1, Pallas kernels: 123 us -> 127 us  [local(): pl.pallas_call(functools.partial(kernel, n), out_shape=pltpu.VMEM(tiles.s...]
where the time goes in v9:
time: 131 us; the launch traced here: 130 us
  Pallas kernels  127 us (97%)
  local copies, waits for them, and re-layouts  1.67 us (1%)
  other arithmetic  1.31 us (1%)
    pallas_call x1, Pallas kernels, local(): pl.pallas_call(functools.partial(kernel, n), out_shape=pltpu.VMEM(tiles.s...  127 us

profile of v9, /device:TPU:1, one launch (start us, length us, event | category | flops | bytes accessed | tf_op | source)
XLA Modules:
  0.0 130.3 jit_solution(8391215643783051010)
XLA Ops:
  0.7 0.7 and_select_fusion
  1.4 0.6 select_reduce_fusion.slot_ref
  2.0 126.6 %shard_map.46 = bf16[16,6,64,256]{3,2,1,0:T(8,128)(2,1)S(1)} custom-call(s32[6,16]{1,0:T(8,128)} %bitcast.3, s32[6,16]{1,0:T(8,128)} %bitcast.4, s32[1]{0:T(128)S(6)} %copy.7.hand_ref, s32[64]{0:T(128)} %select_reduce_fusion.slot_ref, bf16[16,6,64,256]{3,2,1,0:T(8,128)(2,1)} %source_ref.1), custom_call_target="tpu_custom_call" | custom-call | flops 2952790016 | bytes 6291456 | tf_op jit(solution)/shard_map/pallas_call | solution.py:430
  128.6 1.7 %copy.6 = bf16[16,6,64,256]{3,2,1,0:T(8,128)(2,1)} copy(bf16[16,6,64,256]{3,2,1,0:T(8,128)(2,1)S(1)} %shard_map.46) | data formatting | bytes 6291456

commit v10 on v5

--- a/solution.py
+++ b/solution.py
@@ -365,10 +365,10 @@
 
     near_pair(6, False)
     expand(None, (3, 2), False)
-    normalize(1)
     near_pair(7, False)
     expand(None, (1, 0), False)
     start_totals(0)
+    normalize(1)
 
     first = count - hand_ref[0]
 

time: 127 us -> 127 us (level)
  no operation moved by 1% of the time
where the time goes in v10:
time: 127 us
  Pallas kernels  123 us (97%)
  local copies, waits for them, and re-layouts  1.67 us (1%)
  other arithmetic  1.31 us (1%)
    pallas_call x1, Pallas kernels, local(): pl.pallas_call(functools.partial(kernel, n), out_shape=pltpu.VMEM(tiles.s...  123 us

profile of v10, /device:TPU:1, one launch (start us, length us, event | category | flops | bytes accessed | tf_op | source)
XLA Modules:
  0.0 126.6 jit_solution(14117488854136538399)
XLA Ops:
  0.7 0.7 and_select_fusion
  1.4 0.6 select_reduce_fusion.slot_ref
  2.0 122.9 %shard_map.46 = bf16[16,6,64,256]{3,2,1,0:T(8,128)(2,1)S(1)} custom-call(s32[6,16]{1,0:T(8,128)} %bitcast.3, s32[6,16]{1,0:T(8,128)} %bitcast.4, s32[1]{0:T(128)S(6)} %copy.7.hand_ref, s32[64]{0:T(128)} %select_reduce_fusion.slot_ref, bf16[16,6,64,256]{3,2,1,0:T(8,128)(2,1)} %source_ref.1), custom_call_target="tpu_custom_call" | custom-call | flops 2952790016 | bytes 6291456 | tf_op jit(solution)/shard_map/pallas_call | solution.py:431
  124.9 1.7 %copy.6 = bf16[16,6,64,256]{3,2,1,0:T(8,128)(2,1)} copy(bf16[16,6,64,256]{3,2,1,0:T(8,128)(2,1)S(1)} %shard_map.46) | data formatting | bytes 6291456
